TPU v7x, 32 devices: a whole 2x2x4 slice. The times are simulated.
32 devices in a mesh: ifg: 8 (over z, x), tile: 4 (over y, core).
Axes of the slice: x: 2, y: 2, z: 4, core: 2. Of those that a mesh axis runs over, the one named last changes fastest.
Arguments:
- ifgs: bfloat16 [1152, 8, 1024], P('ifg', 'tile'), may hold values from -12 to 12
- pairs: int32 [1152, 2], replicated, may hold values from 0 to 299, as said below
- pseudo_inverse: bfloat16 [300, 1152], P(None, 'ifg'), may hold values from -0.1875 to 0.1875
- ref_pixels: int32 [64], replicated, may hold values from 0 to 8191
- epochs: int32 [8], replicated, may hold values from 8 to 291
Outputs:
- coefficients: float32 [16, 8, 1024], P(None, 'tile', 'ifg')
- misfit_rms: float32 [8, 1024], P('tile', 'ifg')
Inputs may be any that keep to these rules, and one draw needn't show every extreme that they name: pairs[k, 0] < pairs[k, 1] <= pairs[k, 0] + 6.
All inputs are finite; a program needn't handle non-finite values.
Results may differ from a plain program's by a relative error of at most 0.0029.
Values may be sent and summed in bfloat16 or wider, within the bound.
No kernel may reach another device: no remote copies, remote signals or barrier semaphores. Data moves between devices by JAX's collectives and lax.ppermute only.
A program may use at most 64 MiB of HBM per device.

v0:
```python
import math

import jax
import jax.numpy as jnp
from jax import lax
from jax.sharding import PartitionSpec as P

EPS = 1e-06
RIDGE = 1.0


def design(epochs, count):
    index = jnp.arange(count, dtype=jnp.int32)
    days = index.astype(jnp.float32)
    scaled = 2.0 * days / (count - 1) - 1.0
    years = days * 12.0 / 365.25
    smooth = jnp.stack(
        [
            jnp.ones_like(days),
            scaled,
            scaled * scaled,
            scaled * scaled * scaled,
            jnp.sin(2.0 * math.pi * years),
            jnp.cos(2.0 * math.pi * years),
            jnp.sin(4.0 * math.pi * years),
            jnp.cos(4.0 * math.pi * years),
        ],
        axis=1,
    )
    jumps = (index[:, None] >= epochs[None, :]).astype(jnp.float32)
    return jnp.concatenate([smooth, jumps], axis=1)


def fit_operator(epochs, count):
    matrix = design(epochs, count)
    normal = jnp.dot(
        matrix.T, matrix, precision=lax.Precision.HIGHEST, preferred_element_type=jnp.float32
    )
    normal = normal + RIDGE * jnp.eye(matrix.shape[1], dtype=jnp.float32)
    factor = jnp.linalg.cholesky(normal)
    return jax.scipy.linalg.cho_solve((factor, True), matrix.T)


def incidence_matrix(pairs, count):
    dates = jnp.arange(count, dtype=jnp.int32)
    later = (pairs[:, 1:2] == dates[None, :]).astype(jnp.float32)
    earlier = (pairs[:, 0:1] == dates[None, :]).astype(jnp.float32)
    return later - earlier


def shards(ifgs, pairs, pseudo_inverse, ref_pixels, epochs):
    row_count = ifgs.shape[1]
    col_total = ifgs.shape[2]
    col_count = col_total // lax.axis_size("ifg")
    region_size = ref_pixels.shape[0]
    date_count = pseudo_inverse.shape[0]
    tile_index = lax.axis_index("tile")
    ifg_index = lax.axis_index("ifg")
    ref_row = ref_pixels // col_total
    ref_col = ref_pixels % col_total
    row_rel = ref_row - tile_index * row_count
    in_tile = (row_rel >= 0) & (row_rel < row_count)
    row_safe = jnp.clip(row_rel, 0, row_count - 1)
    regrouped = lax.all_to_all(ifgs, "ifg", split_axis=2, concat_axis=0, tiled=True)
    col_rel = ref_col - ifg_index * col_count
    in_block = in_tile & (col_rel >= 0) & (col_rel < col_count)
    col_safe = jnp.clip(col_rel, 0, col_count - 1)
    values = regrouped[:, row_safe, col_safe].astype(jnp.float32)
    partial_value = jnp.sum(jnp.where(in_block[None, :], values, 0.0), axis=1)
    totals = lax.psum(partial_value, ("ifg", "tile"))
    corrected = (regrouped.astype(jnp.float32) - (totals / region_size)[:, None, None]).astype(
        jnp.bfloat16
    )
    pixel_rows = corrected.reshape(corrected.shape[0], row_count * col_count)
    displacement = jnp.dot(
        lax.all_gather(pseudo_inverse, "ifg", axis=1, tiled=True),
        pixel_rows,
        preferred_element_type=jnp.float32,
    )
    operator = fit_operator(epochs, date_count)
    coeffs = jnp.dot(
        operator, displacement, precision=lax.Precision.HIGHEST, preferred_element_type=jnp.float32
    )
    incidence = incidence_matrix(pairs, date_count)
    predicted = jnp.dot(
        incidence, displacement, precision=lax.Precision.HIGHEST, preferred_element_type=jnp.float32
    )
    misfit = pixel_rows.astype(jnp.float32) - predicted
    spread = jnp.sqrt(jnp.mean(misfit * misfit, axis=0) + EPS)
    return (
        coeffs.reshape(operator.shape[0], row_count, col_count),
        spread.reshape(row_count, col_count),
    )


def solution(mesh):
    in_specs = (P("ifg", "tile", None), P(), P(None, "ifg"), P(), P())
    out_specs = (P(None, "tile", "ifg"), P("tile", "ifg"))
    return jax.shard_map(shards, mesh=mesh, in_specs=in_specs, out_specs=out_specs, check_vma=False)
```

profile of v0, /device:TPU:0, one launch (start us, length us, event | category | flops | bytes accessed | tf_op | source)
XLA Modules:
  0.0 109.8 jit_solution(2486271126283309843)
XLA Ops:
  0.6 4.7 %copy.25 = bf16[144,2,1024]{0,1,2:T(2,128)(2,1)} copy(bf16[144,2,1024]{2,1,0:T(2,128)(2,1)} %param.5) | data formatting | bytes 1179648 | tf_op args[0]
  5.3 7.4 %all-to-all-start = ((bf16[144,2,1024]{0,1,2:T(2,128)(2,1)}), bf16[144,2,1024]{0,1,2:T(2,128)(2,1)S(1)}, u32[]{:S(2)}, u32[]{:S(2)}) async-start(bf16[144,2,1024]{0,1,2:T(2,128)(2,1)} %copy.25), calls=%async_computation | async-start | bytes 2097152 | tf_op jit(solution)/shard_map/all_to_all | solution.py:64
  12.7 0.1 fusion.19
  12.8 0.1 fusion.21
  12.9 0.1 multiply_add_fusion
  13.0 0.0 copy-done.2
  13.0 0.1 fusion.10
  13.1 0.2 fusion.35
  13.2 0.1 copy.24
  13.3 1.5 %cholesky.17 = f32[16,16]{1,0:T(8,128)S(1)} custom-call(f32[16,16]{1,0:T(8,128)S(1)} %fusion.17), custom_call_target="Cholesky" | custom-call | tf_op jit(solution)/shard_map/jit(cholesky)/cholesky | solution.py:40
  14.8 0.6 compare_reduce_fusion
  15.4 0.6 fusion.11
  16.1 0.0 copy-done.3
  16.1 0.0 copy-done.1
  16.2 1.2 %custom-call.10 = f32[1,16,16]{1,2,0:T(8,128)S(1)} custom-call(f32[1,16,16]{2,1,0:T(8,128)S(1)} %fusion.11), custom_call_target="InvertDiagBlocksLowerTriangular" | custom-call | tf_op jit(solution)/shard_map/jit(_cho_solve)/triangular_solve | solution.py:41
  17.4 0.2 fusion.14
  17.7 0.2 fusion.12
  17.9 43.9 %all_gather.3 = bf16[300,1152]{0,1:T(8,128)(2,1)S(1)} all-gather(bf16[300,144]{0,1:T(8,128)(2,1)S(1)} %copy-done), channel_id=1, replica_groups=mesh['ifg'=8,'tile'=4] {'ifg'}, dimensions={1}, use_global_device_ids=true | all-gather | bytes 777600 | tf_op jit(solution)/shard_map/all_gather | solution.py:76
  61.7 0.0 all-to-all-done
  61.7 0.8 copy.31
  62.6 1.6 %copy.30 = bf16[144,2,8,128]{3,2,0,1:T(8,128)(2,1)S(1)} copy(bf16[144,2,8,128]{0,1,3,2:T(2,128)(2,1)S(1)} %bitcast.39) | data formatting | bytes 1179648 | tf_op jit(solution)/shard_map/all_to_all | solution.py:64
  64.2 0.3 copy.29
  64.5 1.2 %gather_fusion = bf16[64,1152]{1,0:T(8,128)(2,1)S(1)} fusion(bf16[1152,2,128]{0,2,1:T(8,128)(2,1)S(1)} %copy.29, s32[64]{0:T(128)S(1)} %fusion.25), kind=kCustom, calls=%fused_computation | custom fusion | bytes 295424 | tf_op jit(solution)/shard_map/gather | solution.py:68
  65.7 0.1 select_reduce_fusion
  65.8 38.2 %psum.7 = f32[1152]{0:T(1024)S(1)} all-reduce(f32[1152]{0:T(1024)S(1)} %select_reduce_fusion), channel_id=1, replica_groups=mesh['ifg'=8,'tile'=4] {'ifg','tile'}, use_global_device_ids=true, to_apply=%region_3.4 | all-reduce | flops 1152 | bytes 9216 | tf_op jit(solution)/shard_map/psum | solution.py:70
  104.0 0.1 bitcast_convert_fusion
  104.0 0.9 copy.27
  105.0 0.7 fusion.31
  105.6 0.2 fusion.36
  105.9 0.7 reshape.77
  106.5 2.6 %fusion.4 = f32[256]{0:T(256)S(1)} fusion(f32[256,300]{0,1:T(8,128)S(1)} %fusion.31, s32[1152]{0:T(1024)S(1)} %get-tuple-element.3, s32[1152]{0:T(1024)S(1)} %get-tuple-element.2, f32[1152]{0:T(1024)S(1)} %broadcast_multiply_fusion, f32[144,8,2,128]{3,2,1,0:T(2,128)S(1)} %bitcast.41), kind=kOutput, calls=%fused_computation.8 | convolution fusion | flops 1065180416 | bytes 1501696 | tf_op jit(solution)/shard_map/dot_general | solution.py:85
  109.2 0.6 sqrt_bitcast_fusion
  (14 shorter events, 0.2 us)
Async XLA Ops:
  5.3 7.7 %copy-start.2 = (s32[8]{0:T(128)S(1)}, s32[8]{0:T(128)}, u32[]{:S(2)}) copy-start(s32[8]{0:T(128)} %param.9) | copy-start | bytes 100
  5.3 10.8 %copy-start.3 = (s32[64]{0:T(128)S(1)}, s32[64]{0:T(128)}, u32[]{:S(2)}) copy-start(s32[64]{0:T(128)} %param.8) | copy-start | bytes 772
  5.3 10.8 %copy-start.1 = (s32[1152,2]{0,1:T(2,128)S(1)}, s32[1152,2]{0,1:T(2,128)}, u32[]{:S(2)}) copy-start(s32[1152,2]{0,1:T(2,128)} %param.6) | copy-start | bytes 27652
  5.3 12.5 %copy-start = (bf16[300,144]{0,1:T(8,128)(2,1)S(1)}, bf16[300,144]{0,1:T(8,128)(2,1)}, u32[]{:S(2)}) copy-start(bf16[300,144]{0,1:T(8,128)(2,1)} %param.7) | copy-start | bytes 259204
  5.3 56.4 %all-to-all-start = ((bf16[144,2,1024]{0,1,2:T(2,128)(2,1)}), bf16[144,2,1024]{0,1,2:T(2,128)(2,1)S(1)}, u32[]{:S(2)}, u32[]{:S(2)}) async-start(bf16[144,2,1024]{0,1,2:T(2,128)(2,1)} %copy.25), calls=%async_computation | async-start | bytes 2097152 | tf_op jit(solution)/shard_map/all_to_all | solution.py:64
where the time goes:
time: 110 us
  blocking collectives  82 us (75%)
  local copies, waits for them, and re-layouts  10.3 us (9%)
  starting transfers between devices  7.4 us (7%)
  other arithmetic  5.12 us (5%)
  matrix products  4.07 us (4%)
    all_gather x1, blocking collectives, shards(): lax.all_gather(pseudo_inverse, 'ifg', axis=1, tiled=True)  43.9 us
    psum x1, blocking collectives, shards(): totals = lax.psum(partial_value, ('ifg', 'tile'))  38.2 us
    all_to_all x1, starting transfers between devices, shards(): lax.all_to_all(ifgs, 'ifg', split_axis=2, concat_axis=0, tiled=True)  7.4 us
    unnamed x9, local copies, waits for them, and re-layouts  4.68 us
    all_to_all x3, local copies, waits for them, and re-layouts, shards(): lax.all_to_all(ifgs, 'ifg', split_axis=2, concat_axis=0, tiled=True)  2.79 us
    dot_general x1, matrix products, shards(): jnp.dot(incidence, displacement, precision=lax.Precision.HIGHEST, preferr...  2.65 us
  transfers between devices with their start and end apart: 1, of which 0 were waited for; matrix products, arithmetic and copies ran while one was open for 5% of the time, Pallas kernels for 0%

commit v1 on v0

v1 whole, which is shorter than its diff:
```python
import functools
import math

import jax
import jax.numpy as jnp
from jax import lax
from jax.experimental import pallas as pl
from jax.experimental.pallas import tpu as pltpu
from jax.sharding import PartitionSpec as P

EPS = 1e-06
RIDGE = 1.0
VMEM = pl.BlockSpec(memory_space=pltpu.VMEM)
SMEM = pl.BlockSpec(memory_space=pltpu.SMEM)


def design(epochs, count):
    index = jnp.arange(count, dtype=jnp.int32)
    days = index.astype(jnp.float32)
    scaled = 2.0 * days / (count - 1) - 1.0
    years = days * 12.0 / 365.25
    smooth = jnp.stack(
        [
            jnp.ones_like(days),
            scaled,
            scaled * scaled,
            scaled * scaled * scaled,
            jnp.sin(2.0 * math.pi * years),
            jnp.cos(2.0 * math.pi * years),
            jnp.sin(4.0 * math.pi * years),
            jnp.cos(4.0 * math.pi * years),
        ],
        axis=1,
    )
    jumps = (index[:, None] >= epochs[None, :]).astype(jnp.float32)
    return jnp.concatenate([smooth, jumps], axis=1)


def fit_operator(epochs, count):
    matrix = design(epochs, count)
    normal = jnp.dot(
        matrix.T, matrix, precision=lax.Precision.HIGHEST, preferred_element_type=jnp.float32
    )
    normal = normal + RIDGE * jnp.eye(matrix.shape[1], dtype=jnp.float32)
    factor = jnp.linalg.cholesky(normal)
    return jax.scipy.linalg.cho_solve((factor, True), matrix.T)


def incidence_matrix(pairs, count):
    dates = jnp.arange(count, dtype=jnp.int32)
    later = (pairs[:, 1:2] == dates[None, :]).astype(jnp.bfloat16)
    earlier = (pairs[:, 0:1] == dates[None, :]).astype(jnp.bfloat16)
    return later - earlier


def sums_kernel(row_count, ref_ref, send_ref, out_ref, acc_ref):
    blocks, rows, width = send_ref.shape
    ifg_count = rows // row_count
    cols = blocks * width
    first = lax.axis_index("tile") * row_count
    row = lax.broadcasted_iota(jnp.int32, (8, cols), 0) % row_count + first
    flat = row * cols + lax.broadcasted_iota(jnp.int32, (8, cols), 1)

    def count(i, weight):
        return weight + jnp.where(flat == ref_ref[i], 1.0, 0.0)

    weight = lax.fori_loop(
        0, ref_ref.shape[0], count, jnp.zeros((8, cols), jnp.float32), unroll=8
    )
    acc = jnp.zeros((rows // 8, 8, width), jnp.float32)
    for j in range(blocks):
        values = send_ref[j].astype(jnp.float32).reshape(rows // 8, 8, width)
        acc = acc + values * weight[None, :, j * width : (j + 1) * width]
    acc_ref[...] = acc.reshape(rows, width)
    per_ifg = acc_ref[pl.ds(0, ifg_count, stride=row_count), :]
    for r in range(1, row_count):
        per_ifg = per_ifg + acc_ref[pl.ds(r, ifg_count, stride=row_count), :]
    out_ref[...] = lax.dot_general(
        jnp.ones((8, width), jnp.float32),
        per_ifg,
        (((1,), (1,)), ((), ())),
        precision=lax.Precision.HIGHEST,
        preferred_element_type=jnp.float32,
    )


def partial_sums(ifgs, send, ref_pixels):
    ifg_count, row_count, cols = ifgs.shape
    if send.shape[1] % 16:
        tile = lax.axis_index("tile")
        pixel = jnp.arange(row_count * cols, dtype=jnp.int32) + tile * row_count * cols
        weight = jnp.sum((ref_pixels[:, None] == pixel[None, :]).astype(jnp.float32), axis=0)
        weight = weight.reshape(1, row_count, cols)
        return jnp.sum(ifgs.astype(jnp.float32) * weight, axis=(1, 2))
    sums = pl.pallas_call(
        functools.partial(sums_kernel, row_count),
        out_shape=jax.ShapeDtypeStruct((8, ifg_count), jnp.float32),
        in_specs=[SMEM, VMEM],
        out_specs=VMEM,
        scratch_shapes=[pltpu.VMEM(send.shape[1:], jnp.float32)],
        name="region_sums",
    )(ref_pixels, send)
    return sums[0]


def post_kernel(row_count, recv_ref, mean_ref, inverse_ref, incidence_ref, fit_ref,
                coeff_ref, spread_ref, wide_ref, corr_ref):
    pairs, dates = incidence_ref.shape
    width = recv_ref.shape[1]
    step = 128 if pairs % 128 == 0 else pairs
    for k in range(0, pairs, step):
        wide_ref[...] = recv_ref[row_count * k : row_count * (k + step), :].astype(jnp.float32)
        mean = mean_ref[k : k + step, :]
        for r in range(row_count):
            values = wide_ref[pl.ds(r, step, stride=row_count), :]
            corr_ref[k : k + step, r * width : (r + 1) * width] = (values - mean).astype(
                jnp.bfloat16
            )
    displacement = jnp.dot(
        inverse_ref[...], corr_ref[...], preferred_element_type=jnp.float32
    )
    coeffs = jnp.dot(
        fit_ref[...],
        displacement,
        precision=lax.Precision.HIGHEST,
        preferred_element_type=jnp.float32,
    )
    high = displacement.astype(jnp.bfloat16)
    low = (displacement - high.astype(jnp.float32)).astype(jnp.bfloat16)
    total = jnp.zeros((8, row_count * width), jnp.float32)
    for k in range(0, pairs, step):
        incidence = incidence_ref[k : k + step, :]
        predicted = jnp.dot(incidence, high, preferred_element_type=jnp.float32) + jnp.dot(
            incidence, low, preferred_element_type=jnp.float32
        )
        misfit = corr_ref[k : k + step, :].astype(jnp.float32) - predicted
        total = total + jnp.sum((misfit * misfit).reshape(step // 8, 8, -1), axis=0)
    spread = jnp.sqrt(jnp.sum(total, axis=0, keepdims=True) / pairs + EPS)
    for r in range(row_count):
        coeff_ref[:, r, :] = coeffs[:, r * width : (r + 1) * width]
        spread_ref[r : r + 1, :] = spread[:, r * width : (r + 1) * width]


def swap(array, bit):
    size = lax.axis_size("tile")
    return lax.ppermute(array, "tile", [(i, i ^ bit) for i in range(size)])


def tile_gather(array):
    size = lax.axis_size("tile")
    tile = lax.axis_index("tile")
    parts = [array]
    bit = size // 2
    order = []
    while bit:
        parts = parts + [swap(part, bit) for part in parts]
        order.append(bit)
        bit //= 2
    stacked = jnp.stack(parts)
    offset = [0] * size
    for position in range(size):
        mask = 0
        for place, bit in enumerate(order):
            if position >> place & 1:
                mask |= bit
        offset[mask] = position
    stacked = jnp.stack([parts[offset[m]] for m in range(size)])
    for bit in order:
        swapped = stacked.reshape((size // (2 * bit), 2, bit) + array.shape)
        swapped = jnp.flip(swapped, axis=1).reshape(stacked.shape)
        stacked = jnp.where((tile & bit) != 0, swapped, stacked)
    return stacked


def split_sum(value):
    high = lax.reduce_precision(value, 8, 7)
    middle = lax.reduce_precision(value - high, 8, 7)
    low = lax.reduce_precision(value - high - middle, 8, 7)
    return jnp.stack([high, middle, low]).astype(jnp.bfloat16)


def shards(ifgs, pairs, pseudo_inverse, ref_pixels, epochs):
    ifg_count, row_count, cols = ifgs.shape
    blocks = lax.axis_size("ifg")
    tiles = lax.axis_size("tile")
    width = cols // blocks
    date_count = pseudo_inverse.shape[0]
    pair_count = blocks * ifg_count
    dates = -(-date_count // 16) * 16
    tile = lax.axis_index("tile")

    send = ifgs.reshape(ifg_count, row_count, blocks, width).transpose(2, 0, 1, 3)
    send = send.reshape(blocks, ifg_count * row_count, width)

    share = -(-ifg_count // tiles)
    columns = jnp.pad(pseudo_inverse.T, ((0, share * tiles - ifg_count), (0, 0)))
    columns = lax.dynamic_slice_in_dim(columns, tile * share, share, 0)
    lanes = max(date_count, ifg_count)
    sums = split_sum(partial_sums(ifgs, send, ref_pixels))
    payload = jnp.concatenate(
        [
            jnp.pad(columns, ((0, 0), (0, lanes - date_count))),
            jnp.pad(sums, ((0, 0), (0, lanes - ifg_count))),
        ]
    )
    payload = jnp.broadcast_to(payload[None], (blocks,) + payload.shape)
    payload = lax.all_to_all(payload, "ifg", 0, 0, tiled=True)
    recv = lax.all_to_all(send, "ifg", 0, 0, tiled=True)
    gathered = tile_gather(payload)

    inverse = gathered[:, :, :share, :date_count].transpose(3, 1, 0, 2)
    inverse = inverse.reshape(date_count, blocks, tiles * share)[:, :, :ifg_count]
    inverse = jnp.pad(
        inverse.reshape(date_count, pair_count), ((0, dates - date_count), (0, 0))
    )
    totals = jnp.sum(gathered[:, :, share:, :ifg_count].astype(jnp.float32), axis=(0, 2))
    means = (totals / ref_pixels.shape[0]).reshape(pair_count, 1)
    means = jnp.broadcast_to(means, (pair_count, width))
    incidence = incidence_matrix(pairs, dates)
    fit = jnp.pad(fit_operator(epochs, date_count), ((0, 0), (0, dates - date_count)))

    terms = fit.shape[0]
    return pl.pallas_call(
        functools.partial(post_kernel, row_count),
        out_shape=(
            jax.ShapeDtypeStruct((terms, row_count, width), jnp.float32),
            jax.ShapeDtypeStruct((row_count, width), jnp.float32),
        ),
        in_specs=[VMEM] * 5,
        out_specs=(VMEM, VMEM),
        scratch_shapes=[
            pltpu.VMEM(
                (row_count * (128 if pair_count % 128 == 0 else pair_count), width), jnp.float32
            ),
            pltpu.VMEM((pair_count, row_count * width), jnp.bfloat16),
        ],
        compiler_params=pltpu.CompilerParams(vmem_limit_bytes=32 * 1024 * 1024),
        name="invert",
    )(recv.reshape(pair_count * row_count, width), means, inverse, incidence, fit)


def solution(mesh):
    in_specs = (P("ifg", "tile", None), P(), P(None, "ifg"), P(), P())
    out_specs = (P(None, "tile", "ifg"), P("tile", "ifg"))
    return jax.shard_map(shards, mesh=mesh, in_specs=in_specs, out_specs=out_specs, check_vma=False)
```

time: 110 us -> 50.6 us (0.46)
  blocking collectives: 82 us -> 0 us
  waiting for transfers between devices: 0.01 us -> 9.61 us
  starting transfers between devices: 7.4 us -> 12.4 us
  Pallas kernels: 0 us -> 4.61 us
  other arithmetic: 5.12 us -> 9.69 us
  matrix products: 4.07 us -> 0.54 us
  local copies, waits for them, and re-layouts: 10.3 us -> 12.2 us
    all_gather x1 -> x0, blocking collectives: 43.9 us -> none  [shards(): lax.all_gather(pseudo_inverse, 'ifg', axis=1, tiled=True)]
    psum x1 -> x0, blocking collectives: 38.2 us -> none  [shards(): totals = lax.psum(partial_value, ('ifg', 'tile'))]
    ppermute x0 -> x3, waiting for transfers between devices: none -> 6.33 us  [swap(): return lax.ppermute(array, 'tile', [(i, i ^ bit) for i in range(size)])]
    pallas_call x0 -> x2, Pallas kernels: none -> 4.61 us  [the longest x1 2.31 us: shards(): pl.pallas_call(functools.partial(post_kernel, row_count), out_shape=(jax....]
    dot_general x3 -> x0, matrix products: 3.53 us -> none  [the longest x1 2.65 us: shards(): jnp.dot(incidence, displacement, precision=lax.Precision.HIGHEST, preferr...]
    rev x0 -> x2, local copies, waits for them, and re-layouts: none -> 3.41 us  [tile_gather(): swapped = jnp.flip(swapped, axis=1).reshape(stacked.shape)]
    all_to_all x1 -> x2, starting transfers between devices: 7.4 us -> 10.8 us  [the longest x1 7.25 us: shards(): payload = lax.all_to_all(payload, 'ifg', 0, 0, tiled=True)]
    all_to_all x1 -> x2, waiting for transfers between devices: 0.01 us -> 3.28 us  [the longest x1 3.27 us: shards(): payload = lax.all_to_all(payload, 'ifg', 0, 0, tiled=True)]
  transfers between devices with their start and end apart: 1 -> 5, of which waited for: 0 -> 3; matrix products, arithmetic and copies ran while one was open for 5% -> 33% of each run, Pallas kernels for 0% -> 0%
where the time goes in v1:
time: 50.6 us; the launch traced here: 50 us
  starting transfers between devices  12.4 us (25%)
  local copies, waits for them, and re-layouts  12.2 us (24%)
  other arithmetic  9.69 us (19%)
  waiting for transfers between devices  9.61 us (19%)
  Pallas kernels  4.61 us (9%)
  between operations  0.87 us (2%)
  matrix products  0.54 us (1%)
    all_to_all x1, starting transfers between devices, shards(): payload = lax.all_to_all(payload, 'ifg', 0, 0, tiled=True)  7.25 us
    ppermute x3, waiting for transfers between devices, swap(): return lax.ppermute(array, 'tile', [(i, i ^ bit) for i in range(size)])  6.33 us
    all_to_all x1, starting transfers between devices, shards(): recv = lax.all_to_all(send, 'ifg', 0, 0, tiled=True)  3.54 us
    rev x2, local copies, waits for them, and re-layouts, tile_gather(): swapped = jnp.flip(swapped, axis=1).reshape(stacked.shape)  3.41 us
    all_to_all x1, waiting for transfers between devices, shards(): payload = lax.all_to_all(payload, 'ifg', 0, 0, tiled=True)  3.27 us
    select_n x2, other arithmetic, tile_gather(): stacked = jnp.where(tile & bit != 0, swapped, stacked)  2.85 us
    another operation x2, local copies, waits for them, and re-layouts, shards(): inverse.reshape(date_count, pair_count)  2.84 us
    unnamed x14, local copies, waits for them, and re-layouts  2.48 us
  transfers between devices with their start and end apart: 5, of which 3 were waited for; matrix products, arithmetic and copies ran while one was open for 33% of the time, Pallas kernels for 0%

profile of v1, /device:TPU:0, one launch (start us, length us, event | category | flops | bytes accessed | tf_op | source)
XLA Modules:
  0.0 50.0 jit_solution(13089173448572115085)
XLA Ops:
  0.6 1.1 %copy-done = bf16[144,2,1024]{2,1,0:T(2,128)(2,1)S(1)} copy-done((bf16[144,2,1024]{2,1,0:T(2,128)(2,1)S(1)}, bf16[144,2,1024]{2,1,0:T(2,128)(2,1)}, u32[]{:S(2)}) %copy-start) | copy-done | bytes 589848
  1.7 1.2 %copy_bitcast_fusion = bf16[144,2,8,128]{3,1,0,2:T(2,128)(2,1)} fusion(bf16[144,2,1024]{2,1,0:T(2,128)(2,1)S(1)} %copy-done), kind=kLoop, calls=%fused_computation.10 | loop fusion | bytes 1179648 | tf_op jit(solution)/shard_map/reshape | solution.py:192
  2.9 2.3 %region_sums.1 = f32[8,144]{1,0:T(8,128)} custom-call(s32[64]{0:T(128)} %ref_ref.1, bf16[8,288,128]{2,1,0:T(8,128)(2,1)} %bitcast.1.send_ref), custom_call_target="tpu_custom_call" | custom-call | tf_op jit(solution)/shard_map/region_sums/pallas_call | solution.py:95
  5.2 0.7 %reduce-precision_convert_fusion.1 = (bf16[1,144]{1,0:T(2,128)(2,1)S(1)}, bf16[1,144]{1,0:T(2,128)(2,1)S(1)}, bf16[1,144]{1,0:T(2,128)(2,1)S(1)}) fusion(f32[8,144]{1,0:T(8,128)} %region_sums.1), kind=kLoop, calls=%fused_computation.49 | loop fusion | flops 1152 | bytes 1440 | tf_op jit(solution)/shard_map/convert
  5.9 0.8 %dynamic-slice_bitcast_fusion = bf16[36,300]{1,0:T(8,128)(2,1)S(1)} fusion(bf16[300,144]{0,1:T(8,128)(2,1)} %param.7, s32[]{:T(128)S(6)} %select_n.34), kind=kLoop, calls=%fused_computation.13 | loop fusion | bytes 43204 | tf_op jit(solution)/shard_map/dynamic_slice | solution.py:197
  6.8 0.7 %broadcast_in_dim.5 = bf16[8,39,300]{2,1,0:T(8,128)(2,1)} broadcast(bf16[39,300]{1,0:T(8,128)(2,1)S(1)} %pad_maximum_fusion.1), dimensions={1,2} | broadcast | bytes 210600 | tf_op jit(solution)/shard_map/broadcast_in_dim | solution.py:206
  7.5 7.3 %all-to-all-start.1 = ((bf16[8,39,300]{2,1,0:T(8,128)(2,1)}), bf16[8,39,300]{2,1,0:T(8,128)(2,1)S(1)}, u32[]{:S(2)}, u32[]{:S(2)}) async-start(bf16[8,39,300]{2,1,0:T(8,128)(2,1)} %broadcast_in_dim.5), calls=%async_computation.1 | async-start | bytes 491520 | tf_op jit(solution)/shard_map/all_to_all | solution.py:207
  15.1 0.2 fusion.25
  15.3 1.5 %cholesky.17 = f32[16,16]{1,0:T(8,128)S(1)} custom-call(f32[16,16]{1,0:T(8,128)S(1)} %fusion.11), custom_call_target="Cholesky" | custom-call | tf_op jit(solution)/shard_map/jit(cholesky)/cholesky | solution.py:45
  16.8 0.6 %compare_reduce_fusion = pred[]{:T(512)} fusion(f32[16]{0:T(128)S(1)} %select_reduce_fusion), kind=kLoop, calls=%fused_computation.38 | loop fusion | flops 31 | bytes 65 | tf_op jit(solution)/shard_map/jit(cholesky)/cholesky | solution.py:45
  17.5 0.6 %fusion.5 = f32[1,16,16]{2,1,0:T(8,128)S(1)} fusion(f32[16,16]{1,0:T(8,128)S(1)} %cholesky.17, pred[]{:T(512)} %compare_reduce_fusion), kind=kLoop, calls=%fused_computation.17 | loop fusion | flops 1024 | bytes 2049 | tf_op jit(solution)/shard_map/jit(_cho_solve)/triangular_solve | solution.py:46
  18.1 1.2 %custom-call.10 = f32[1,16,16]{1,2,0:T(8,128)S(1)} custom-call(f32[1,16,16]{2,1,0:T(8,128)S(1)} %fusion.5), custom_call_target="InvertDiagBlocksLowerTriangular" | custom-call | tf_op jit(solution)/shard_map/jit(_cho_solve)/triangular_solve | solution.py:46
  19.4 0.7 %fusion.3.incidence_ref = bf16[1152,304]{1,0:T(8,128)(2,1)S(1)} fusion(s32[1152]{0:T(1024)S(1)} %get-tuple-element.3, s32[1152]{0:T(1024)S(1)} %get-tuple-element.2), kind=kLoop, calls=%fused_computation.8 | loop fusion | flops 2801664 | bytes 709632 | tf_op jit(solution)/shard_map/sub | solution.py:53
  20.1 3.3 %all-to-all-done.1 = bf16[8,39,300]{2,1,0:T(8,128)(2,1)S(1)} async-done(((bf16[8,39,300]{2,1,0:T(8,128)(2,1)}), bf16[8,39,300]{2,1,0:T(8,128)(2,1)S(1)}, u32[]{:S(2)}, u32[]{:S(2)}) %all-to-all-start.1) | async-done | bytes 187232 | tf_op jit(solution)/shard_map/all_to_all | solution.py:207
  23.4 3.5 %all-to-all-start = ((bf16[8,288,128]{2,1,0:T(8,128)(2,1)}), bf16[8,288,128]{2,1,0:T(8,128)(2,1)S(1)}, u32[]{:S(2)}, u32[]{:S(2)}) async-start(bf16[8,288,128]{2,1,0:T(8,128)(2,1)} %bitcast.1.send_ref), calls=%async_computation | async-start | bytes 1179648 | tf_op jit(solution)/shard_map/all_to_all | solution.py:208
  27.0 1.6 %collective-permute-start.1 = (bf16[8,39,300]{2,0,1:T(8,128)(2,1)S(1)}, bf16[8,39,300]{2,0,1:T(8,128)(2,1)S(1)}, u32[]{:S(2)}, u32[]{:S(2)}) collective-permute-start(bf16[8,39,300]{2,0,1:T(8,128)(2,1)S(1)} %copy.18), channel_id=1, source_target_pairs={{0,2},{1,3},{2,0},{3,1},{4,6},{5,7},{6,4},{7,5},{8,10},{9,11},{10,... | collective-permute-start | bytes 561608 | tf_op jit(solution)/shard_map/ppermute | solution.py:146
  28.6 0.2 fusion.8
  28.9 5.1 %collective-permute-done.1 = bf16[8,39,300]{2,0,1:T(8,128)(2,1)S(1)} collective-permute-done((bf16[8,39,300]{2,0,1:T(8,128)(2,1)S(1)}, bf16[8,39,300]{2,0,1:T(8,128)(2,1)S(1)}, u32[]{:S(2)}, u32[]{:S(2)}) %collective-permute-start.1) | collective-permute-done | bytes 187232 | tf_op jit(solution)/shard_map/ppermute | solution.py:146
  33.9 0.2 fusion.6
  34.2 1.3 %collective-permute-done.2 = bf16[8,39,300]{2,0,1:T(8,128)(2,1)S(1)} collective-permute-done((bf16[8,39,300]{2,0,1:T(8,128)(2,1)S(1)}, bf16[8,39,300]{2,0,1:T(8,128)(2,1)S(1)}, u32[]{:S(2)}, u32[]{:S(2)}) %collective-permute-start.2) | collective-permute-done | bytes 187232 | tf_op jit(solution)/shard_map/ppermute | solution.py:146
  35.4 0.2 pad_maximum_fusion
  35.7 0.4 copy-done.4
  36.1 1.2 %bitcast_select_fusion.1 = bf16[2,2,1,8,39,300]{5,3,4,1,0,2:T(8,128)(2,1)} fusion(bf16[2,2,1,8,39,300]{5,3,4,1,0,2:T(8,128)(2,1)S(1)} %bitcast.50, pred[]{:T(512)S(6)} %ne.7, bf16[1,2,2,8,39,300]{5,3,4,2,1,0:T(8,128)(2,1)S(1)} %bitcast.49), kind=kLoop, calls=%fused_computation.7 | loop fusion | flops 374400 | bytes 2246401 | tf_op jit(solution)/shard_map/jit(_where)/select_n | solution.py:171
  37.3 1.0 %rev.8 = bf16[1,2,2,8,39,300]{5,3,4,2,1,0:T(8,128)(2,1)} reverse(bf16[1,2,2,8,39,300]{5,3,4,2,1,0:T(8,128)(2,1)S(1)} %bitcast.51), dimensions={1} | reverse | bytes 1497600 | tf_op jit(solution)/shard_map/jit(_flip)/rev | solution.py:170
  38.4 2.4 %rev.9 = bf16[2,2,1,8,39,300]{5,3,4,1,0,2:T(8,128)(2,1)} reverse(bf16[2,2,1,8,39,300]{5,3,4,1,0,2:T(8,128)(2,1)} %bitcast_select_fusion.1), dimensions={1} | reverse | bytes 1497600 | tf_op jit(solution)/shard_map/jit(_flip)/rev | solution.py:170
  40.8 1.7 %fusion.2 = bf16[4,8,39,300]{3,1,2,0:T(8,128)(2,1)S(1)} fusion(bf16[1,2,2,8,39,300]{5,3,4,2,1,0:T(8,128)(2,1)S(1)} %copy-done.1, bf16[2,2,1,8,39,300]{5,3,4,1,0,2:T(8,128)(2,1)} %rev.9, pred[]{:T(512)S(6)} %ne.7, pred[]{:T(512)S(6)} %ne.6, bf16[1,8,39,300]{3,1,2,0:T(8,128)(2,1)} %bitcast.59, bf16[1,8,39,300]{3,1,2,0:T(8,128)(2,1)S(1)} %bitcast.55, ...), kind=kLoop, calls=%fused_computation.6 | loop fusion | flops 1872000 | bytes 2995202 | tf_op jit(solution)/shard_map/jit(_where)/select_n | solution.py:171
  42.4 1.0 %copy-done.2 = bf16[4,8,39,300]{3,1,2,0:T(8,128)(2,1)} copy-done((bf16[4,8,39,300]{3,1,2,0:T(8,128)(2,1)}, bf16[4,8,39,300]{3,1,2,0:T(8,128)(2,1)S(1)}, u32[]{:S(2)}) %copy-start.2) | copy-done | bytes 748824
  43.6 1.3 %reshape_reshape.3 = bf16[300,1152]{0,1:T(8,128)(2,1)} reshape(bf16[300,8,4,36]{0,3,2,1:T(8,128)(2,1)S(1)} %copy.21) | data formatting | bytes 1382400 | tf_op jit(solution)/shard_map/reshape;reshape | solution.py:214
  44.9 1.5 %copy.22 = bf16[300,1152]{1,0:T(8,128)(2,1)S(1)} copy(bf16[300,1152]{0,1:T(8,128)(2,1)} %reshape_reshape.3) | data formatting | bytes 1382400 | tf_op jit(solution)/shard_map/reshape;reshape | solution.py:214
  46.5 0.8 %convert_reduce_fusion = f32[8,144]{1,0:T(8,128)S(1)} fusion(bf16[4,8,39,300]{3,1,2,0:T(8,128)(2,1)} %copy-done.2), kind=kLoop, calls=%fused_computation.11 | loop fusion | flops 26496 | bytes 32256 | tf_op jit(solution)/shard_map/reduce_sum | solution.py:216
  47.5 0.2 broadcast_in_dim.6.mean_ref
  47.7 2.3 %invert.1 = (f32[16,2,128]{2,1,0:T(2,128)}, f32[2,128]{1,0:T(2,128)}) custom-call(bf16[2304,128]{1,0:T(8,128)(2,1)S(1)} %bitcast.48, f32[1152,128]{1,0:T(8,128)S(1)} %broadcast_in_dim.6.mean_ref, bf16[304,1152]{1,0:T(8,128)(2,1)S(1)} %pad.13.inverse_ref, bf16[1152,304]{1,0:T(8,128)(2,1)S(1)} %fusion.3.incidence_ref, f32[16,304]{1,0:T(8,128)S(1)} %pad.14.fit_ref), custom_call_target="tpu_custom_call" | custom-call | tf_op jit(solution)/shard_map/invert/pallas_call | solution.py:223
  (36 shorter events, 1.0 us)
Async XLA Ops:
  0.6 1.1 %copy-start = (bf16[144,2,1024]{2,1,0:T(2,128)(2,1)S(1)}, bf16[144,2,1024]{2,1,0:T(2,128)(2,1)}, u32[]{:S(2)}) copy-start(bf16[144,2,1024]{2,1,0:T(2,128)(2,1)} %param.5) | copy-start | bytes 1769476
  2.9 12.1 %copy-start.6 = (s32[8]{0:T(128)S(1)}, s32[8]{0:T(128)}, u32[]{:S(2)}) copy-start(s32[8]{0:T(128)} %param.9) | copy-start | bytes 100
  2.9 16.4 %copy-start.5 = (s32[1152,2]{0,1:T(2,128)S(1)}, s32[1152,2]{0,1:T(2,128)}, u32[]{:S(2)}) copy-start(s32[1152,2]{0,1:T(2,128)} %param.6) | copy-start | bytes 27652
  7.5 15.9 %all-to-all-start.1 = ((bf16[8,39,300]{2,1,0:T(8,128)(2,1)}), bf16[8,39,300]{2,1,0:T(8,128)(2,1)S(1)}, u32[]{:S(2)}, u32[]{:S(2)}) async-start(bf16[8,39,300]{2,1,0:T(8,128)(2,1)} %broadcast_in_dim.5), calls=%async_computation.1 | async-start | bytes 491520 | tf_op jit(solution)/shard_map/all_to_all | solution.py:207
  23.4 24.0 %all-to-all-start = ((bf16[8,288,128]{2,1,0:T(8,128)(2,1)}), bf16[8,288,128]{2,1,0:T(8,128)(2,1)S(1)}, u32[]{:S(2)}, u32[]{:S(2)}) async-start(bf16[8,288,128]{2,1,0:T(8,128)(2,1)} %bitcast.1.send_ref), calls=%async_computation | async-start | bytes 1179648 | tf_op jit(solution)/shard_map/all_to_all | solution.py:208
  27.0 6.9 %collective-permute-start.1 = (bf16[8,39,300]{2,0,1:T(8,128)(2,1)S(1)}, bf16[8,39,300]{2,0,1:T(8,128)(2,1)S(1)}, u32[]{:S(2)}, u32[]{:S(2)}) collective-permute-start(bf16[8,39,300]{2,0,1:T(8,128)(2,1)S(1)} %copy.18), channel_id=1, source_target_pairs={{0,2},{1,3},{2,0},{3,1},{4,6},{5,7},{6,4},{7,5},{8,10},{9,11},{10,... | collective-permute-start | bytes 561608 | tf_op jit(solution)/shard_map/ppermute | solution.py:146
  28.8 5.4 %collective-permute-start = (bf16[8,39,300]{2,0,1:T(8,128)(2,1)S(1)}, bf16[8,39,300]{2,0,1:T(8,128)(2,1)S(1)}, u32[]{:S(2)}, u32[]{:S(2)}) collective-permute-start(bf16[8,39,300]{2,0,1:T(8,128)(2,1)S(1)} %copy.18), channel_id=1, source_target_pairs={{0,1},{1,0},{2,3},{3,2},{4,5},{5,4},{6,7},{7,6},{8,9},{9,8},{10,11... | collective-permute-start | bytes 561608 | tf_op jit(solution)/shard_map/ppermute | solution.py:146
  33.9 1.5 %collective-permute-start.2 = (bf16[8,39,300]{2,0,1:T(8,128)(2,1)S(1)}, bf16[8,39,300]{2,0,1:T(8,128)(2,1)S(1)}, u32[]{:S(2)}, u32[]{:S(2)}) collective-permute-start(bf16[8,39,300]{2,0,1:T(8,128)(2,1)S(1)} %collective-permute-done.1), channel_id=1, source_target_pairs={{0,1},{1,0},{2,3},{3,2},{4,5},{5,4},{6,7},{7,6},{8,9},{9,8},{10,11... | collective-permute-start | bytes 561608 | tf_op jit(solution)/shard_map/ppermute | solution.py:146
  34.2 1.3 %copy-start.3 = (bf16[8,39,300]{2,0,1:T(8,128)(2,1)}, bf16[8,39,300]{2,0,1:T(8,128)(2,1)S(1)}, u32[]{:S(2)}) copy-start(bf16[8,39,300]{2,0,1:T(8,128)(2,1)S(1)} %collective-permute-done) | copy-start | bytes 561604
  35.4 0.7 %copy-start.4 = (bf16[8,39,300]{2,0,1:T(8,128)(2,1)}, bf16[8,39,300]{2,0,1:T(8,128)(2,1)S(1)}, u32[]{:S(2)}) copy-start(bf16[8,39,300]{2,0,1:T(8,128)(2,1)S(1)} %collective-permute-done.2) | copy-start | bytes 561604
  38.4 2.4 %copy-start.1 = (bf16[1,2,2,8,39,300]{5,3,4,2,1,0:T(8,128)(2,1)S(1)}, bf16[1,2,2,8,39,300]{5,3,4,2,1,0:T(8,128)(2,1)}, u32[]{:S(2)}) copy-start(bf16[1,2,2,8,39,300]{5,3,4,2,1,0:T(8,128)(2,1)} %rev.8) | copy-start | bytes 2246404
  42.4 1.0 %copy-start.2 = (bf16[4,8,39,300]{3,1,2,0:T(8,128)(2,1)}, bf16[4,8,39,300]{3,1,2,0:T(8,128)(2,1)S(1)}, u32[]{:S(2)}) copy-start(bf16[4,8,39,300]{3,1,2,0:T(8,128)(2,1)S(1)} %fusion.2) | copy-start | bytes 2246404
